TPU v7x, 256 devices: a whole 4x4x8 slice. The times are simulated.
256 devices in a mesh: sub: 2 (over core), row: 16 (over y, x), col: 8 (over z).
Axes of the slice: x: 4, y: 4, z: 8, core: 2. Of those that a mesh axis runs over, the one named last changes fastest.
Arguments:
- front: bfloat16 [2048, 102400], P('row', ('sub', 'col')), may hold values from -6 to 6
- child_update: bfloat16 [2048, 131072], P('row', ('sub', 'col')), may hold values from -6 to 6
- col_map: int32 [1024], P(('sub', 'col')), may hold values from 0 to 799, as said below
- pivots: int32 [2, 512], replicated, may hold values from 0 to 511, each once within a row
- diag_inverse: float32 [2, 512, 512], replicated, may hold values from -0.01171875 to 0.01171875
- ranks: int32 [2, 16], P(None, 'row'), may hold values from 1 to 64
- bases: bfloat16 [64, 2048], P(None, 'row'), may hold values from -0.5 to 0.5
Outputs:
- front_out: bfloat16 [2048, 102400], P('row', ('sub', 'col'))
- coefficients: bfloat16 [2, 16, 64, 512], P(None, 'row')
Inputs may be any that keep to these rules, and one draw needn't show every extreme that they name: `col_map`: within each half of the array (one child) the values are distinct. Each aligned run of 64 entries (one device's blocks) holds, for every o from 0 to 15, exactly 4 values v with o * 50 <= v < (o + 1) * 50.
All inputs are finite; a program needn't handle non-finite values.
Results may differ from a plain program's by a relative error of at most 0.011.
Values may be sent and summed in bfloat16 or wider, within the bound.
A program may use at most 128 MiB of HBM per device.

v0:
```python
import jax
import jax.numpy as jnp
from jax import lax
from jax.sharding import PartitionSpec as P

BS = 128
P_SIZE = 512
NPAN = 2
RMAX = 64


def spread(value, axis, source):
    kept = jnp.where(lax.axis_index(axis) == source, value, 0).astype(value.dtype)
    return lax.psum(kept, axis)


def compress(panel_cols, inverse, rank_basis):
    row_count = panel_cols.shape[0]
    lower = jnp.dot(panel_cols, inverse, precision=lax.Precision.HIGHEST)
    blocked = lower.reshape(row_count // BS, BS, P_SIZE)
    return jnp.einsum(
        "rnb,nbp->nrp", rank_basis.astype(jnp.float32), blocked, precision=lax.Precision.HIGHEST
    ).astype(jnp.bfloat16)


def local(front, child_update, col_map, pivots, diag_inverse, ranks, bases):
    row_count, local_cols = front.shape
    local_blocks = local_cols // BS
    child_blocks = col_map.shape[0]
    target = col_map // local_blocks
    arrange = jnp.argsort(target, stable=True)
    places = (col_map % local_blocks)[arrange].reshape(1, child_blocks)
    outgoing = child_update.reshape(row_count, child_blocks, BS)[:, arrange, :].reshape(
        row_count, child_blocks * BS
    )
    direct_rows, direct_places = (
        lax.all_to_all(outgoing, ("sub", "col"), split_axis=1, concat_axis=1, tiled=True),
        lax.all_to_all(places, ("sub", "col"), split_axis=1, concat_axis=1, tiled=True),
    )
    received = direct_rows.reshape(row_count, child_blocks, BS)
    positions = direct_places.reshape(child_blocks)
    selector = (positions[:, None] == jnp.arange(local_blocks, dtype=jnp.int32)[None, :]).astype(
        jnp.bfloat16
    )
    added = jnp.einsum("rmb,mp->rpb", received, selector, preferred_element_type=jnp.float32)
    front_work = front.astype(jnp.float32) + added.reshape(row_count, local_cols)
    global_rows = lax.axis_index("row") * row_count + jnp.arange(row_count, dtype=jnp.int32)
    row_blocks = row_count // BS
    row_span = min(row_count, P_SIZE)
    coefficient_list = []
    for step in range(NPAN):
        offset = step * P_SIZE % local_cols
        owner_index = step * P_SIZE // local_cols
        rank_mask = (jnp.arange(RMAX, dtype=jnp.int32)[:, None] < ranks[step][None, :]).astype(
            jnp.bfloat16
        )
        rank_basis = bases.reshape(RMAX, row_blocks, BS) * rank_mask[:, :, None]
        panel_cols = front_work[:, offset : offset + P_SIZE]
        shared_cols = spread(panel_cols, ("sub", "col"), owner_index)
        coefficients = compress(shared_cols, diag_inverse[step], rank_basis)
        row_offset = step * P_SIZE % row_count
        source_rows = front_work.astype(jnp.bfloat16)
        first_root = step * P_SIZE // row_count
        pieces = []
        for counter in range(P_SIZE // row_span):
            pieces.append(spread(source_rows, "row", first_root + counter))
        pivot_block = jnp.concatenate(pieces, axis=0)
        upper = jnp.take(pivot_block, pivots[step], axis=0)
        reduced = jnp.einsum(
            "nrp,pc->nrc", coefficients, upper, preferred_element_type=jnp.float32
        ).astype(jnp.bfloat16)
        update = jnp.einsum(
            "rnb,nrc->nbc", rank_basis, reduced, preferred_element_type=jnp.float32
        ).reshape(row_count, local_cols)
        below = (global_rows >= (step + 1) * P_SIZE)[:, None]
        front_work = front_work - jnp.where(below, update, jnp.float32(0.0))
        coefficient_list.append(coefficients)
    return (front_work.astype(jnp.bfloat16), jnp.stack(coefficient_list))


def solution(mesh):
    return jax.shard_map(
        local,
        mesh=mesh,
        in_specs=(
            P("row", ("sub", "col")),
            P("row", ("sub", "col")),
            P(("sub", "col")),
            P(),
            P(),
            P(None, "row"),
            P(None, "row"),
        ),
        out_specs=(P("row", ("sub", "col")), P(None, "row", None, None)),
        check_vma=False,
    )
```

profile of v0, /device:TPU:56, one launch (start us, length us, event | category | flops | bytes accessed | tf_op | source)
XLA Modules:
  0.0 672.4 jit_solution(10603311928575517583)
XLA Ops:
  7.2 0.7 and_select_fusion.1
  7.8 2.0 sort.17
  9.9 0.8 gather_fusion
  10.7 0.7 all_to_all.12
  11.4 8.6 %all-to-all-start = ((s32[1,16,4]{2,0,1:T(1,128)}), s32[1,16,4]{2,0,1:T(1,128)S(1)}, u32[]{:S(2)}, u32[]{:S(2)}) async-start(s32[1,16,4]{2,0,1:T(1,128)} %bitcast), calls=%async_computation | async-start | bytes 16384 | tf_op jit(solution)/shard_map/all_to_all | solution.py:38
  19.9 4.1 copy.18
  24.0 3.2 copy.19
  27.2 2.1 gather_fusion.1
  29.4 4.1 copy.20
  33.5 0.0 all-to-all-done
  33.5 7.2 %all-to-all-start.1 = ((bf16[128,16,512]{0,2,1:T(8,128)(2,1)}), bf16[128,16,512]{0,2,1:T(8,128)(2,1)S(1)}, u32[]{:S(2)}, u32[]{:S(2)}) async-start(bf16[128,16,512]{0,2,1:T(8,128)(2,1)} %bitcast.4), calls=%async_computation.1 | async-start | bytes 4194304 | tf_op jit(solution)/shard_map/all_to_all | solution.py:37
  40.7 0.0 all-reduce.7.cloned.1.call-start
  40.7 0.5 broadcast.66
  41.3 0.7 reduce.3
  41.9 0.1 eq.45
  42.0 47.0 %all-to-all-done.1 = bf16[128,16,512]{0,2,1:T(8,128)(2,1)S(1)} async-done(((bf16[128,16,512]{0,2,1:T(8,128)(2,1)}), bf16[128,16,512]{0,2,1:T(8,128)(2,1)S(1)}, u32[]{:S(2)}, u32[]{:S(2)}) %all-to-all-start.1) | async-done | bytes 2097184 | tf_op jit(solution)/shard_map/all_to_all | solution.py:37
  89.1 0.0 copy-start
  89.1 1.3 copy-done
  90.4 3.3 copy.24
  93.7 2.4 convolution_bitcast_fusion
  96.1 3.7 copy.22
  99.9 3.2 copy.23
  103.0 4.5 broadcast_select_fusion.7
  107.6 0.7 slice_select_fusion.1
  108.3 0.0 all-reduce.7.cloned.1.call-update
  108.3 0.0 all-reduce.13.cloned.1.call-start
  108.4 3.7 broadcast_select_fusion.6
  112.1 0.0 copy-start.5
  112.1 0.0 copy-start.4
  112.1 0.0 copy-start.3
  112.1 0.0 all-reduce.13.cloned.1.call-update
  112.2 0.2 all-reduce.9.cloned.1.call-start
  112.4 0.4 copy-done.5
  112.8 0.6 fusion.37
  113.4 0.6 compare_convert_fusion.1
  114.0 0.0 copy-done.4
  114.1 99.6 %all-reduce.7.cloned.1.call-done = f32[128,512]{1,0:T(8,128)} async-done(((f32[128,512]{1,0:T(8,128)}), f32[128,512]{1,0:T(8,128)}) %all-reduce.7.cloned.1.call-update) | async-done | bytes 262160 | tf_op jit(solution)/shard_map/psum | solution.py:14
  213.7 2.0 fusion.13
  215.7 0.0 copy-done.3
  215.7 0.3 convolution_convert_fusion.3
  216.0 140.3 %all-reduce.13.cloned.1.call-done = (bf16[128,6400]{1,0:T(8,128)(2,1)}, bf16[128,6400]{1,0:T(8,128)(2,1)}, bf16[128,6400]{1,0:T(8,128)(2,1)}, bf16[128,6400]{1,0:T(8,128)(2,1)}) async-done(((bf16[128,6400]{1,0:T(8,128)(2,1)}, bf16[128,6400]{1,0:T(8,128)(2,1)}, bf16[128,6400]{1,0:T(8,128)(2,1)}, bf16[128,6400]{1,0:T(8,128)(2,1)}), (bf16[128,6400]{1,0:T(8,128)(2,1)}, bf16[128,6400]{1,0:T(8,128)(2,1)}, ...) | async-done | bytes 6553616 | tf_op jit(solution)/shard_map/psum | solution.py:14
  356.3 6.6 pad_maximum_fusion
  362.8 16.3 %gather_fusion.2 = bf16[512,6400]{1,0:T(8,128)(2,1)} fusion(bf16[512,6400]{1,0:T(8,128)(2,1)} %pad_maximum_fusion, s32[1024]{0:T(1024)S(1)} %pad_clamp_fusion.1), kind=kCustom, calls=%fused_computation.clone | custom fusion | bytes 13109248 | tf_op jit(solution)/shard_map/jit(_take)/gather | solution.py:68
  379.1 7.5 %broadcast_select_fusion.3 = (bf16[128,6400]{1,0:T(8,128)(2,1)}, bf16[128,6400]{1,0:T(8,128)(2,1)}, f32[128,6400]{1,0:T(8,128)}) fusion(pred[]{:T(512)S(6)} %eq.54, f32[128,6400]{1,0:T(8,128)S(1)} %get-tuple-element.17, bf16[64,512]{1,0:T(8,128)(2,1)S(1)} %convolution_convert_fusion.3, bf16[512,6400]{1,0:T(8,128)(2,1)} %gather_fusion.2, ...), kind=kOutput, calls=%fused_computation.24 | convolution fusion | flops 531259392 | bytes 16466689 | tf_op jit(solution)/shard_map/rnb,nrc->nbc/dot_general | solution.py:72
  386.6 1.7 slice_select_fusion
  388.3 0.0 all-reduce.9.cloned.1.call-update
  388.3 0.3 all-reduce.11.cloned.1.call-start
  388.6 3.7 broadcast_select_fusion.2
  392.3 0.0 copy-start.2
  392.3 0.0 all-reduce.11.cloned.1.call-update
  392.3 0.8 compare_convert_fusion
  393.2 101.3 %all-reduce.9.cloned.1.call-done = f32[128,512]{1,0:T(8,128)} async-done(((f32[128,512]{1,0:T(8,128)}), f32[128,512]{1,0:T(8,128)}) %all-reduce.9.cloned.1.call-update) | async-done | bytes 262160 | tf_op jit(solution)/shard_map/psum | solution.py:14
  494.5 0.0 copy-done.2
  494.5 1.7 fusion.11
  496.2 0.3 convolution_convert_fusion.2
  496.4 0.7 pad_maximum_fusion.2
  497.1 139.9 %all-reduce.11.cloned.1.call-done = (bf16[128,6400]{1,0:T(8,128)(2,1)}, bf16[128,6400]{1,0:T(8,128)(2,1)}, bf16[128,6400]{1,0:T(8,128)(2,1)}, bf16[128,6400]{1,0:T(8,128)(2,1)}) async-done(((bf16[128,6400]{1,0:T(8,128)(2,1)}, bf16[128,6400]{1,0:T(8,128)(2,1)}, bf16[128,6400]{1,0:T(8,128)(2,1)}, bf16[128,6400]{1,0:T(8,128)(2,1)}), (bf16[128,6400]{1,0:T(8,128)(2,1)}, bf16[128,6400]{1,0:T(8,128)(2,1)}, ...) | async-done | bytes 6553616 | tf_op jit(solution)/shard_map/psum | solution.py:14
  637.0 6.6 pad_maximum_fusion.1
  643.6 0.0 copy-start.1
  643.6 16.4 %gather_fusion.3 = bf16[512,6400]{1,0:T(8,128)(2,1)} fusion(bf16[512,6400]{1,0:T(8,128)(2,1)} %pad_maximum_fusion.1, s32[1024]{0:T(1024)S(1)} %pad_clamp_fusion), kind=kCustom, calls=%fused_computation.1.clone | custom fusion | bytes 13109248 | tf_op jit(solution)/shard_map/jit(_take)/gather | solution.py:68
  660.0 0.0 copy-done.1
  660.0 5.9 fusion.2
  (12 shorter events, 0.1 us)
Async XLA Ops:
  11.4 22.1 %all-to-all-start = ((s32[1,16,4]{2,0,1:T(1,128)}), s32[1,16,4]{2,0,1:T(1,128)S(1)}, u32[]{:S(2)}, u32[]{:S(2)}) async-start(s32[1,16,4]{2,0,1:T(1,128)} %bitcast), calls=%async_computation | async-start | bytes 16384 | tf_op jit(solution)/shard_map/all_to_all | solution.py:38
  33.5 55.6 %all-to-all-start.1 = ((bf16[128,16,512]{0,2,1:T(8,128)(2,1)}), bf16[128,16,512]{0,2,1:T(8,128)(2,1)S(1)}, u32[]{:S(2)}, u32[]{:S(2)}) async-start(bf16[128,16,512]{0,2,1:T(8,128)(2,1)} %bitcast.4), calls=%async_computation.1 | async-start | bytes 4194304 | tf_op jit(solution)/shard_map/all_to_all | solution.py:37
  40.7 173.0 %all-reduce.7.cloned.1.call-start = ((), (), s32[]{:S(2)}) async-start(), calls=%async_computation.2 | async-start | bytes 524288 | tf_op jit(solution)/shard_map/psum | solution.py:14
  89.1 1.3 copy-start
  108.3 247.9 %all-reduce.13.cloned.1.call-start = ((), (), s32[]{:S(2)}) async-start(), calls=%async_computation.5 | async-start | bytes 13107200 | tf_op jit(solution)/shard_map/psum | solution.py:14
  112.1 0.7 copy-start.5
  112.1 1.9 copy-start.4
  112.1 103.6 %copy-start.3 = (bf16[64,128]{1,0:T(8,128)(2,1)S(1)}, bf16[64,128]{1,0:T(8,128)(2,1)}, u32[]{:S(2)}) copy-start(bf16[64,128]{1,0:T(8,128)(2,1)} %param.15) | copy-start | bytes 49156
  112.2 382.4 %all-reduce.9.cloned.1.call-start = ((), (), s32[]{:S(2)}) async-start(), calls=%async_computation.3 | async-start | bytes 524288 | tf_op jit(solution)/shard_map/psum | solution.py:14
  388.3 248.7 %all-reduce.11.cloned.1.call-start = ((), (), s32[]{:S(2)}) async-start(), calls=%async_computation.4 | async-start | bytes 13107200 | tf_op jit(solution)/shard_map/psum | solution.py:14
  392.3 102.2 %copy-start.2 = (f32[2,512,512]{2,1,0:T(8,128)S(1)}, f32[2,512,512]{2,1,0:T(8,128)}, u32[]{:S(2)}) copy-start(f32[2,512,512]{2,1,0:T(8,128)} %param.13) | copy-start | bytes 6291460
  643.6 16.4 %copy-start.1 = (f32[128,6400]{1,0:T(8,128)S(1)}, f32[128,6400]{1,0:T(8,128)}, u32[]{:S(2)}) copy-start(f32[128,6400]{1,0:T(8,128)} %get-tuple-element.30) | copy-start | bytes 9830404
Sparse Core Ops, SparseCore 0:
  108.5 105.1 all-reduce.6
  218.3 137.8 all-reduce.12
  388.4 106.0 all-reduce.8
  499.0 137.9 all-reduce.10
where the time goes:
time: 675 us; the launch traced here: 672 us
  waiting for transfers between devices  528 us (78%)
  local copies, waits for them, and re-layouts  60.8 us (9%)
  other arithmetic  33.1 us (5%)
  matrix products  20 us (3%)
  starting transfers between devices  16.4 us (2%)
  between operations  14 us (2%)
    psum x4, waiting for transfers between devices, spread(): return lax.psum(kept, axis)  481 us
    all_to_all x1, waiting for transfers between devices, local(): lax.all_to_all(outgoing, ('sub', 'col'), split_axis=1, concat_axis=1, til...  47 us
    gather x2, local copies, waits for them, and re-layouts, local(): upper = jnp.take(pivot_block, pivots[step], axis=0)  32.7 us
    select_n x5, other arithmetic, spread(): jnp.where(lax.axis_index(axis) == source, value, 0).astype(value.dtype)  14.4 us
  transfers between devices with their start and end apart: 6, of which 5 were waited for; matrix products, arithmetic and copies ran while one was open for 4% of the time, Pallas kernels for 0%

commit v1 on v0

v1 whole, which is shorter than its diff:
```python
import functools

import jax
import jax.numpy as jnp
from jax import lax
from jax.experimental import pallas as pl
from jax.experimental.pallas import tpu as pltpu
from jax.sharding import PartitionSpec as P

BS = 128
PW = 512
RM = 64
ROWS = 128
COLS = 6400
PB = 50
KB = 64
NO = 16
ZS = 8
NCH = 4
RC = ROWS // NCH
WORKERS = (0, 1, 2, 3, 8, 9, 10, 11, 12, 13)
NW = len(WORKERS)
WC = COLS // NW
F32 = jnp.float32
BF16 = jnp.bfloat16
HIGH = lax.Precision.HIGHEST


def nt(a, b):
    return lax.dot_general(a, b, (((1,), (1,)), ((), ())), preferred_element_type=F32)


def mm(a, b):
    return jnp.dot(a, b, preferred_element_type=F32)


def mm_high(a, b):
    return jnp.dot(a, b, preferred_element_type=F32, precision=HIGH)


def transposed(a):
    return a.astype(F32).T


def kernel(
    cm, piv, ranks, bases, child, front, inv, out, coef_out,
    child_v, childs, front_v, inv_v, outbuf, recvs, plc_out, plc_in, arr_v, arr_s, src_v, src_s,
    work, fb, p1, u0p, coef, gmsg, g0, g1, u, r0, r1, rbuf, outv,
    s_child, s_load, s_idx, sa, ra, sp, rp, su, ru, sc, rcv, sg, rg, ss, rs, sr, rr, so, s_coef, s_self,
):
    s, r, c = lax.axis_index("sub"), lax.axis_index("row"), lax.axis_index("col")
    o = s * ZS + c

    def at_owner(q):
        return {"sub": q // ZS, "col": lax.rem(q, ZS)}

    def at_row(i):
        return {"row": jnp.int32(i)}

    def remote(src, dst, send, recv, dev):
        return pltpu.make_async_remote_copy(
            src_ref=src, dst_ref=dst, send_sem=send, recv_sem=recv, device_id=dev,
            device_id_type=pl.DeviceIdType.MESH,
        )

    def arrived(dst, sem):
        pltpu.make_async_copy(dst, dst, sem).wait()

    loads = []
    for ch in range(NCH):
        rows = pl.ds(ch * RC, RC)
        loads.append(pltpu.make_async_copy(child.at[rows, :], child_v.at[ch], s_child.at[ch]))
        loads[-1].start()
    front_load = pltpu.make_async_copy(front, front_v, s_load.at[0])
    front_load.start()
    inv_load = pltpu.make_async_copy(inv, inv_v, s_load.at[1])
    inv_load.start()

    barrier = pltpu.get_barrier_semaphore()

    @pl.loop(1, 16)
    def _(k):
        pl.semaphore_signal(
            barrier, inc=1, device_id=at_owner(lax.rem(o + k, NO)), device_id_type=pl.DeviceIdType.MESH
        )
        pl.semaphore_signal(
            barrier, inc=1, device_id=at_row(lax.rem(r + k, 16)), device_id_type=pl.DeviceIdType.MESH
        )

    i0 = lax.broadcasted_iota(jnp.int32, (KB, KB), 0)
    i1 = lax.broadcasted_iota(jnp.int32, (KB, KB), 1)
    along = jnp.broadcast_to(cm[...], (KB, KB))
    down = jnp.sum(jnp.where(i0 == i1, along, 0), axis=1, keepdims=True)
    t_along = (along * 1311) >> 16
    t_down = (down * 1311) >> 16
    slot = jnp.sum(jnp.where((t_along == t_down) & (i1 < i0), 1, 0), axis=1, keepdims=True)
    match = (4 * t_down + slot) == i1
    arrange = jnp.max(jnp.where(match, i0, 0), axis=0, keepdims=True)
    places = jnp.sum(jnp.where(match, down - PB * t_down, 0), axis=0, keepdims=True)
    arr_v[...] = jnp.zeros_like(arr_v)
    arr_v[:, 0:KB] = jnp.broadcast_to(arrange, (8, KB))
    plc_out[...] = jnp.zeros_like(plc_out)
    plc_out[:, 0:KB] = jnp.broadcast_to(places, (8, KB))
    idx_load = pltpu.make_async_copy(arr_v, arr_s, s_idx.at[0])
    idx_load.start()
    plc_in[o] = plc_out[...]
    for ch in range(NCH):
        recvs[ch][0] = jnp.zeros((RC, BS), BF16)
    idx_load.wait()
    pl.semaphore_wait(barrier, 30)

    def send_places(q):
        return remote(plc_out, plc_in.at[o], sp.at[q], rp.at[o], at_owner(q))

    def send_blocks(ch, q):
        return remote(
            outbuf.at[ch, pl.ds(4 * q, 4)], recvs[ch].at[pl.ds(1 + 4 * o, 4)], sa.at[ch, q], ra.at[ch, o],
            at_owner(q),
        )

    def pack(ch, q):
        for j in range(4):
            outbuf[ch, 4 * q + j] = childs[ch][arr_s[0, 4 * q + j]]

    @pl.loop(1, NO)
    def _(k):
        send_places(lax.rem(o + k, NO)).start()

    for ch in range(NCH):
        loads[ch].wait()

        @pl.loop(0, KB, unroll=8)
        def _(j, ch=ch):
            childs[ch][j] = child_v[ch, :, pl.ds(pl.multiple_of(j * BS, BS), BS)]

    for ch in range(NCH):
        pack(ch, 0)

        @pl.when(o != 0)
        def _(ch=ch):
            send_blocks(ch, 0).start()

    for ch in range(NCH):

        @pl.loop(0, NO)
        def _(t, ch=ch):
            step = t // 2
            shift = jnp.where(lax.rem(step, 2) == 1, (step + 1) // 2, ZS - step // 2)
            q = lax.rem(s + lax.rem(t, 2), 2) * ZS + lax.rem(c + shift, ZS)

            @pl.when(q != 0)
            def _():
                pack(ch, q)

                @pl.when(q != o)
                def _():
                    send_blocks(ch, q).start()

        for j in range(4):
            recvs[ch][1 + 4 * o + j] = outbuf[ch, 4 * o + j]

    @pl.loop(1, NO)
    def _(k):
        q = lax.rem(o + k, NO)
        arrived(plc_in.at[q], rp.at[q])

    ip = lax.broadcasted_iota(jnp.int32, (56, BS), 0)
    lane = lax.broadcasted_iota(jnp.int32, (56, BS), 1)
    mine = (lane >= 4 * o) & (lane < 4 * o + 4)
    for half in range(2):
        found = jnp.zeros((56, BS), jnp.int32)
        for q in range(half * ZS, (half + 1) * ZS):
            hit = mine & (plc_in[q, 0:1, :] == ip)
            found = jnp.maximum(found, jnp.where(hit, 4 * q + 1 + lane - 4 * o, 0))
        src_v[half] = jnp.broadcast_to(jnp.max(found, axis=1, keepdims=True), (56, BS))
    src_load = pltpu.make_async_copy(src_v, src_s, s_idx.at[1])
    src_load.start()
    front_load.wait()
    src_load.wait()

    def add_blocks(ch, first, last):
        rows = pl.ds(ch * RC, RC)

        @pl.loop(first, last)
        def _(p):
            at = pl.ds(pl.multiple_of(p * BS, BS), BS)
            one = recvs[ch][src_s[0, p, 0]].astype(F32)
            two = recvs[ch][src_s[1, p, 0]].astype(F32)
            total = front_v[rows, at].astype(F32) + one + two
            work[rows, at] = total
            fb[rows, at] = total.astype(BF16)

    def wait_blocks(ch):
        @pl.loop(1, NO)
        def _(k):
            q = lax.rem(o + k, NO)
            arrived(recvs[ch].at[pl.ds(1 + 4 * q, 4)], ra.at[ch, q])

    def send_rows(ch, w):
        src = fb.at[pl.ds(ch * RC, RC), pl.ds(w * WC, WC)]
        dst = u.at[pl.ds(pl.multiple_of(r * ROWS + ch * RC, RC), RC), :]
        return src, dst

    def scatter(ch):
        for w, row in enumerate(WORKERS):
            src, dst = send_rows(ch, w)

            @pl.when((r < 8) & (r == row))
            def _():
                pltpu.make_async_copy(src, dst, rs.at[ch, lax.rem(r, 8)]).start()

            @pl.when((r < 8) & (r != row))
            def _():
                remote(src, dst, ss.at[ch, w], rs.at[ch, lax.rem(r, 8)], at_row(row)).start()

    rank_row = lax.broadcasted_iota(jnp.int32, (RM, BS), 0)

    def basis(k):
        return jnp.where(rank_row < ranks[k, 0], bases[...].astype(F32), 0.0)

    def order(k):
        ids = lax.broadcasted_iota(jnp.int32, (PW, PW), 0)
        one_hot = jnp.where(piv[k : k + 1, :] == ids, 1.0, 0.0).astype(BF16)
        gmsg[k, :, 0:PW] = nt(coef[k], one_hot).astype(BF16)
        gmsg[k, :, PW : PW + BS] = basis(k).astype(BF16)

    def send_coef(k, q):
        return remote(coef.at[k], coef.at[k], sc.at[k, q], rcv.at[k], at_owner(q))

    def send_panel(i):
        return remote(
            fb.at[:, pl.ds(PW, PW)], u0p.at[pl.ds(pl.multiple_of(lax.rem(r, 4) * ROWS, ROWS), ROWS), :],
            su.at[i], ru.at[lax.rem(r, 4)], at_row(i),
        )

    @pl.when(o == 0)
    def _():
        for ch in range(NCH):
            wait_blocks(ch)
        for ch in range(NCH):
            add_blocks(ch, 0, 8)

        @pl.when(r < 4)
        def _():
            for i in range(4, 16):
                send_panel(i).start()

        inv_load.wait()
        coef[0] = mm_high(mm_high(basis(0), work[:, 0:PW]), inv_v[0]).astype(BF16)

        @pl.loop(1, NO)
        def _(q):
            send_coef(0, q).start()

        order(0)
        for ch in range(NCH):
            add_blocks(ch, 8, PB)
        for ch in range(NCH):
            scatter(ch)

        p1[...] = work[:, PW : 2 * PW]

        @pl.when(r >= 4)
        def _():
            for i in range(4):
                arrived(u0p.at[pl.ds(i * ROWS, ROWS), :], ru.at[i])
            reduced = mm(gmsg[0, :, 0:PW], u0p[...]).astype(BF16)
            p1[...] = p1[...] - mm(transposed(basis(0)).astype(BF16), reduced)

        coef[1] = mm_high(mm_high(basis(1), p1[...]), inv_v[1]).astype(BF16)

        @pl.loop(1, NO)
        def _(q):
            send_coef(1, q).start()

        order(1)

    @pl.when(o != 0)
    def _():
        inv_load.wait()
        arrived(coef.at[0], rcv.at[0])
        order(0)

    def send_order(k, w):
        first = 4 * (k + 1)
        at = pl.ds(pl.multiple_of(jnp.maximum(r - first, 0) * RM, RM), RM)
        return gmsg.at[k], (g0, g1)[k].at[at, :]

    def share(k):
        for w, row in enumerate(WORKERS):
            src, dst = send_order(k, w)

            @pl.when((r >= 4 * (k + 1)) & (r == row))
            def _():
                pltpu.make_async_copy(src, dst, rg.at[k, r]).start()

            @pl.when((r >= 4 * (k + 1)) & (r != row))
            def _():
                remote(src, dst, sg.at[k, w], rg.at[k, r], at_row(row)).start()

    share(0)

    @pl.when(o != 0)
    def _():
        arrived(coef.at[1], rcv.at[1])
        order(1)

    share(1)
    coef_copy = pltpu.make_async_copy(coef, coef_out, s_coef)
    coef_copy.start()

    @pl.when(o != 0)
    def _():
        for ch in range(NCH):
            wait_blocks(ch)
            add_blocks(ch, 0, PB)
            scatter(ch)

    w_me = jnp.int32(0)
    is_worker = r < 0
    for w, row in enumerate(WORKERS):
        w_me = jnp.where(r == row, w, w_me)
        is_worker = is_worker | (r == row)
    my_cols = pl.ds(pl.multiple_of(w_me * WC, BS), WC)

    def send_reduced(k, i):
        src = (r0, r1)[k].at[pl.ds((i - 4 * (k + 1)) * RM, RM), :]
        dst = rbuf.at[pl.ds(k * RM, RM), my_cols]
        return src, dst

    def give(k):
        for i in range(4 * (k + 1), 16):
            src, dst = send_reduced(k, i)

            @pl.when(r == i)
            def _():
                pltpu.make_async_copy(src, dst, rr.at[k, w_me]).start()

            @pl.when(r != i)
            def _():
                remote(src, dst, sr.at[k, i], rr.at[k, w_me], at_row(i)).start()

    @pl.when(is_worker)
    def _():
        for i in range(4, 16):
            arrived(g0.at[pl.ds((i - 4) * RM, RM), :], rg.at[0, i])
        for ch in range(NCH):
            for i in range(4):
                arrived(u.at[pl.ds(i * ROWS + ch * RC, RC), :], rs.at[ch, i])

        @pl.loop(0, 3)
        def _(t):
            at = pl.ds(pl.multiple_of(t * 256, 256), 256)
            r0[at, :] = mm(g0[at, 0:PW], u[0:PW, :]).astype(BF16)

        give(0)
        for ch in range(NCH):
            for i in range(4, 8):
                arrived(u.at[pl.ds(i * ROWS + ch * RC, RC), :], rs.at[ch, i])
        for i in range(4):
            b_t = transposed(g0[i * RM : (i + 1) * RM, PW : PW + BS]).astype(BF16)
            rows = pl.ds(PW + i * ROWS, ROWS)
            change = mm(b_t, r0[i * RM : (i + 1) * RM, :])
            u[rows, :] = (u[rows, :].astype(F32) - change).astype(BF16)
        for i in range(8, 16):
            arrived(g1.at[pl.ds((i - 8) * RM, RM), :], rg.at[1, i])

        @pl.loop(0, 2)
        def _(t):
            at = pl.ds(pl.multiple_of(t * 256, 256), 256)
            r1[at, :] = mm(g1[at, 0:PW], u[PW : 2 * PW, :]).astype(BF16)

        give(1)

    def write(w, src):
        at = pl.ds(w * WC, WC)
        return pltpu.make_async_copy(src.at[:, at], out.at[:, at], so.at[w])

    @pl.when(r < 4)
    def _():
        for w in range(NW):
            write(w, fb).start()

    @pl.when((r >= 4) & (r < 8))
    def _():
        b_t = transposed(basis(0)).astype(BF16)
        for w in range(NW):
            at = pl.ds(w * WC, WC)
            arrived(rbuf.at[pl.ds(0, RM), at], rr.at[0, w])
            outv[:, at] = (work[:, at] - mm(b_t, rbuf[0:RM, at])).astype(BF16)
            write(w, outv).start()

    @pl.when(r >= 8)
    def _():
        b_t = transposed(jnp.concatenate([basis(0), basis(1)], axis=0)).astype(BF16)
        for w in range(NW):
            at = pl.ds(w * WC, WC)
            for k in range(2):
                arrived(rbuf.at[pl.ds(k * RM, RM), at], rr.at[k, w])
            outv[:, at] = (work[:, at] - mm(b_t, rbuf[:, at])).astype(BF16)
            write(w, outv).start()

    for w in range(NW):
        write(w, outv).wait()
    coef_copy.wait()

    @pl.loop(1, NO)
    def _(k):
        q = lax.rem(o + k, NO)
        send_places(q).wait_send()
        for ch in range(NCH):
            send_blocks(ch, q).wait_send()

        @pl.when(o == 0)
        def _():
            for j in range(2):
                send_coef(j, q).wait_send()

    @pl.when((o == 0) & (r < 4))
    def _():
        for i in range(4, 16):
            send_panel(i).wait_send()

    for w, row in enumerate(WORKERS):
        for ch in range(NCH):
            src, dst = send_rows(ch, w)

            @pl.when((r < 8) & (r != row))
            def _():
                remote(src, dst, ss.at[ch, w], rs.at[ch, lax.rem(r, 8)], at_row(row)).wait_send()

        for k in range(2):
            src, dst = send_order(k, w)

            @pl.when((r >= 4 * (k + 1)) & (r != row))
            def _():
                remote(src, dst, sg.at[k, w], rg.at[k, r], at_row(row)).wait_send()

    for k in range(2):
        for i in range(4 * (k + 1), 16):
            src, dst = send_reduced(k, i)

            @pl.when(is_worker & (r != i))
            def _():
                remote(src, dst, sr.at[k, i], rr.at[k, w_me], at_row(i)).wait_send()


def local(front, child_update, col_map, pivots, diag_inverse, ranks, bases):
    vmem, smem, anywhere = (
        pl.BlockSpec(memory_space=pltpu.VMEM), pl.BlockSpec(memory_space=pltpu.SMEM),
        pl.BlockSpec(memory_space=pl.ANY),
    )
    dma = pltpu.SemaphoreType.DMA
    scratch = [
        pltpu.VMEM((NCH, RC, KB * BS), BF16),
        [pltpu.VMEM((KB, RC, BS), BF16) for _ in range(NCH)],
        pltpu.VMEM((ROWS, COLS), BF16),
        pltpu.VMEM((2, PW, PW), F32),
        pltpu.VMEM((NCH, KB, RC, BS), BF16),
        [pltpu.VMEM((KB + 1, RC, BS), BF16) for _ in range(NCH)],
        pltpu.VMEM((8, BS), jnp.int32),
        pltpu.VMEM((NO, 8, BS), jnp.int32),
        pltpu.VMEM((8, BS), jnp.int32),
        pltpu.SMEM((8, BS), jnp.int32),
        pltpu.VMEM((2, 56, BS), jnp.int32),
        pltpu.SMEM((2, 56, BS), jnp.int32),
        pltpu.VMEM((ROWS, COLS), F32),
        pltpu.VMEM((ROWS, COLS), BF16),
        pltpu.VMEM((ROWS, PW), F32),
        pltpu.VMEM((PW, PW), BF16),
        pltpu.VMEM((2, RM, PW), BF16),
        pltpu.VMEM((2, RM, PW + BS), BF16),
        pltpu.VMEM((12 * RM, PW + BS), BF16),
        pltpu.VMEM((8 * RM, PW + BS), BF16),
        pltpu.VMEM((2 * PW, WC), BF16),
        pltpu.VMEM((12 * RM, WC), BF16),
        pltpu.VMEM((8 * RM, WC), BF16),
        pltpu.VMEM((2 * RM, COLS), BF16),
        pltpu.VMEM((ROWS, COLS), BF16),
        dma((NCH,)), dma((2,)), dma((2,)),
        dma((NCH, NO)), dma((NCH, NO)), dma((NO,)), dma((NO,)),
        dma((16,)), dma((4,)),
        dma((2, NO)), dma((2,)),
        dma((2, NW)), dma((2, 16)),
        dma((NCH, NW)), dma((NCH, 8)),
        dma((2, 16)), dma((2, NW)),
        dma((NW,)), dma(()), dma(()),
    ]
    front_out, coefficients = pl.pallas_call(
        kernel,
        out_shape=(
            jax.ShapeDtypeStruct((ROWS, COLS), BF16),
            jax.ShapeDtypeStruct((2, RM, PW), BF16),
        ),
        in_specs=[vmem, vmem, smem, vmem, anywhere, anywhere, anywhere],
        out_specs=(anywhere, anywhere),
        scratch_shapes=scratch,
        compiler_params=pltpu.CompilerParams(
            collective_id=0, has_side_effects=True, vmem_limit_bytes=50 * 1024 * 1024
        ),
        cost_estimate=pl.CostEstimate(flops=1_200_000_000, bytes_accessed=8_000_000, transcendentals=0),
    )(col_map.reshape(1, KB), pivots, ranks, bases, child_update, front, diag_inverse)
    return front_out, coefficients.reshape(2, 1, RM, PW)


def solution(mesh):
    return jax.shard_map(
        local,
        mesh=mesh,
        in_specs=(
            P("row", ("sub", "col")),
            P("row", ("sub", "col")),
            P(("sub", "col")),
            P(),
            P(),
            P(None, "row"),
            P(None, "row"),
        ),
        out_specs=(P("row", ("sub", "col")), P(None, "row", None, None)),
        check_vma=False,
    )
```

time: 675 us -> 139 us (0.21)
  the two profiles are of different devices: /device:TPU:56 before, /device:TPU:159 now
where the time goes in v1:
time: 139 us
  Pallas kernels  132 us (95%)
  local copies, waits for them, and re-layouts  6.05 us (4%)
    pallas_call x1, Pallas kernels, local(): pl.pallas_call(kernel, out_shape=(jax.ShapeDtypeStruct((ROWS, COLS), BF16...  132 us
    unnamed x11, local copies, waits for them, and re-layouts  6.05 us

profile of v1, /device:TPU:159, one launch (start us, length us, event | category | flops | bytes accessed | tf_op | source)
XLA Modules:
  0.0 138.8 jit_solution(4634542103293109214)
XLA Ops:
  0.6 0.7 copy.9.ranks
  1.4 0.0 copy-start
  1.4 1.4 %copy-done = bf16[128,6400]{1,0:T(8,128)(2,1)S(1)} copy-done((bf16[128,6400]{1,0:T(8,128)(2,1)S(1)}, bf16[128,6400]{1,0:T(8,128)(2,1)}, u32[]{:S(2)}) %copy-start) | copy-done | bytes 1638424
  2.8 0.0 copy-start.1
  2.8 0.7 copy-done.1
  3.5 0.0 copy-start.2
  3.5 0.7 copy-done.2
  4.2 0.0 copy-start.3
  4.2 0.7 copy-done.3
  4.9 132.1 %shard_map.86 = (bf16[128,6400]{1,0:T(8,128)(2,1)S(1)}, bf16[2,64,512]{2,1,0:T(8,128)(2,1)S(1)}) custom-call(s32[1,64]{1,0:T(1,128)S(1)} %bitcast.5, s32[2,512]{1,0:T(2,128)S(1)} %copy-done.2, s32[2,1]{1,0:T(2,128)S(1)} %copy.9.ranks, bf16[64,128]{1,0:T(8,128)(2,1)S(1)} %copy-done.1, bf16[128,8192]{1,0:T(8,128)(2,1)} %child.1, ...), custom_call_target="tpu_custom_call" | custom-call | flops 1200000000 | bytes 8000000 | tf_op jit(solution)/shard_map/pallas_call | solution.py:489
  137.0 1.2 copy.13
  138.1 0.7 copy.14
Async XLA Ops:
  1.4 1.4 %copy-start = (bf16[128,6400]{1,0:T(8,128)(2,1)S(1)}, bf16[128,6400]{1,0:T(8,128)(2,1)}, u32[]{:S(2)}) copy-start(bf16[128,6400]{1,0:T(8,128)(2,1)} %front.1) | copy-start | bytes 4915204
  2.8 0.7 copy-start.1
  3.5 0.7 copy-start.2
  4.2 0.7 copy-start.3

commit v2 on v1

v2 whole, which is shorter than its diff:
```python
import functools

import jax
import jax.numpy as jnp
from jax import lax
from jax.experimental import pallas as pl
from jax.experimental.pallas import tpu as pltpu
from jax.sharding import PartitionSpec as P

BS = 128
PW = 512
RM = 64
ROWS = 128
COLS = 6400
PB = 50
KB = 64
NO = 16
ZS = 8
NCH = 4
RC = ROWS // NCH
NW = 16
SHARES = ((0, 2, 3), (2, 8, 2), (8, 16, 4))
WC = 4 * BS
F32 = jnp.float32
BF16 = jnp.bfloat16
HIGH = lax.Precision.HIGHEST


def first_col(w):
    return pl.multiple_of(jnp.where(w < 8, 2 * w + jnp.minimum(w, 2), 4 * w - 14) * BS, BS)


def by_width(w, act):
    for start, end, blocks in SHARES:

        @pl.when((w >= start) & (w < end))
        def _():
            act(blocks * BS)


def nt(a, b):
    return lax.dot_general(a, b, (((1,), (1,)), ((), ())), preferred_element_type=F32)


def mm(a, b):
    return jnp.dot(a, b, preferred_element_type=F32)


def mm_high(a, b):
    return jnp.dot(a, b, preferred_element_type=F32, precision=HIGH)


def transposed(a):
    return a.astype(F32).T


def kernel(
    cm_h, piv_h, ranks_h, bases_h, child, front, inv, out, coef_out,
    cm, piv, ranks, bases, one_hot, child_v, childs, front_v, inv_v, outbuf, recvs, plc_out, plc_in, arr_v, arr_s, src_v, src_s,
    work, fb, p1, u0p, coef, gm0, gm1, g0, g1, u, r0, r1, rbuf, outv,
    s_child, s_load, s_idx, sa, ra, sp, rp, su, ru, sc, rcv, sg, rg, sf, ss, rs, sr, rr, so, s_coef,
):
    s, r, c = lax.axis_index("sub"), lax.axis_index("row"), lax.axis_index("col")
    o = s * ZS + c

    def at_owner(q):
        return {"sub": q // ZS, "col": lax.rem(q, ZS)}

    def at_row(i):
        return {"row": i}

    def remote(src, dst, send, recv, dev):
        return pltpu.make_async_remote_copy(
            src_ref=src, dst_ref=dst, send_sem=send, recv_sem=recv, device_id=dev,
            device_id_type=pl.DeviceIdType.MESH,
        )

    def arrived(dst, sem):
        pltpu.make_async_copy(dst, dst, sem).wait()

    small = []
    for i, (src, dst) in enumerate(((cm_h, cm), (piv_h, piv), (ranks_h, ranks), (bases_h, bases))):
        small.append(pltpu.make_async_copy(src, dst, s_load.at[2 + i]))
        small[-1].start()
    loads = []
    for ch in range(NCH):
        rows = pl.ds(ch * RC, RC)
        loads.append(pltpu.make_async_copy(child.at[rows, :], child_v.at[ch], s_child.at[ch]))
        loads[-1].start()
    front_load = pltpu.make_async_copy(front, front_v, s_load.at[0])
    front_load.start()
    inv_load = pltpu.make_async_copy(inv, inv_v, s_load.at[1])
    inv_load.start()

    barrier = pltpu.get_barrier_semaphore()

    @pl.loop(1, 16)
    def _(k):
        pl.semaphore_signal(
            barrier, inc=1, device_id=at_owner(lax.rem(o + k, NO)), device_id_type=pl.DeviceIdType.MESH
        )
        pl.semaphore_signal(
            barrier, inc=1, device_id=at_row(lax.rem(r + k, 16)), device_id_type=pl.DeviceIdType.MESH
        )

    small[0].wait()
    i0 = lax.broadcasted_iota(jnp.int32, (KB, KB), 0)
    i1 = lax.broadcasted_iota(jnp.int32, (KB, KB), 1)
    along = jnp.broadcast_to(cm[...], (KB, KB))
    down = jnp.sum(jnp.where(i0 == i1, along, 0), axis=1, keepdims=True)
    t_along = (along * 1311) >> 16
    t_down = (down * 1311) >> 16
    slot = jnp.sum(jnp.where((t_along == t_down) & (i1 < i0), 1, 0), axis=1, keepdims=True)
    match = (4 * t_down + slot) == i1
    arrange = jnp.max(jnp.where(match, i0, 0), axis=0, keepdims=True)
    places = jnp.sum(jnp.where(match, down - PB * t_down, 0), axis=0, keepdims=True)
    arr_v[...] = jnp.zeros_like(arr_v)
    arr_v[:, 0:KB] = jnp.broadcast_to(arrange, (8, KB))
    plc_out[...] = jnp.zeros_like(plc_out)
    plc_out[:, 0:KB] = jnp.broadcast_to(places, (8, KB))
    idx_load = pltpu.make_async_copy(arr_v, arr_s, s_idx.at[0])
    idx_load.start()
    plc_in[o] = plc_out[...]
    for ch in range(NCH):
        recvs[ch][0] = jnp.zeros((RC, BS), BF16)
    idx_load.wait()
    pl.semaphore_wait(barrier, 30)

    def send_places(q):
        return remote(plc_out, plc_in.at[o], sp.at[q], rp.at[o], at_owner(q))

    def send_blocks(ch, q):
        return remote(
            outbuf.at[ch, pl.ds(4 * q, 4)], recvs[ch].at[pl.ds(1 + 4 * o, 4)], sa.at[ch, q], ra.at[ch, o],
            at_owner(q),
        )

    def pack(ch, q):
        for j in range(4):
            outbuf[ch, 4 * q + j] = childs[ch][arr_s[0, 4 * q + j]]

    @pl.loop(1, NO)
    def _(k):
        send_places(lax.rem(o + k, NO)).start()

    for ch in range(NCH):
        loads[ch].wait()

        @pl.loop(0, KB, unroll=8)
        def _(j, ch=ch):
            childs[ch][j] = child_v[ch, :, pl.ds(pl.multiple_of(j * BS, BS), BS)]

    def send_chunk(ch):
        @pl.loop(0, NO)
        def _(t):
            if ch == 0:

                @pl.when(lax.rem(t, 4) == 0)
                def _():
                    for early in range(NCH):

                        @pl.when(t == 4 * early)
                        def _():
                            pack(early, 0)

                            @pl.when(o != 0)
                            def _():
                                send_blocks(early, 0).start()

            step = t // 2
            shift = jnp.where(lax.rem(step, 2) == 1, (step + 1) // 2, ZS - step // 2)
            q = lax.rem(s + lax.rem(t, 2), 2) * ZS + lax.rem(c + shift, ZS)

            @pl.when(q != 0)
            def _():
                pack(ch, q)

                @pl.when(q != o)
                def _():
                    send_blocks(ch, q).start()

        for j in range(4):
            recvs[ch][1 + 4 * o + j] = outbuf[ch, 4 * o + j]

    send_chunk(0)

    @pl.when(o == 0)
    def _():
        for ch in range(1, NCH):
            for j in range(4):
                recvs[ch][1 + j] = outbuf[ch, j]

    send_chunk(1)

    @pl.when(o != 0)
    def _():
        send_chunk(2)
        send_chunk(3)

    for load in small[1:]:
        load.wait()
    ids = lax.broadcasted_iota(jnp.int32, (PW, PW), 0)
    for k in range(2):
        one_hot[k] = jnp.where(piv[k : k + 1, :] == ids, 1.0, 0.0).astype(BF16)

    @pl.loop(1, NO)
    def _(k):
        q = lax.rem(o + k, NO)
        arrived(plc_in.at[q], rp.at[q])

    ip = lax.broadcasted_iota(jnp.int32, (56, BS), 0)
    lane = lax.broadcasted_iota(jnp.int32, (56, BS), 1)
    mine = (lane >= 4 * o) & (lane < 4 * o + 4)
    for half in range(2):
        found = jnp.zeros((56, BS), jnp.int32)
        for q in range(half * ZS, (half + 1) * ZS):
            hit = mine & (plc_in[q, 0:1, :] == ip)
            found = jnp.maximum(found, jnp.where(hit, 4 * q + 1 + lane - 4 * o, 0))
        src_v[half] = jnp.broadcast_to(jnp.max(found, axis=1, keepdims=True), (56, BS))
    src_load = pltpu.make_async_copy(src_v, src_s, s_idx.at[1])
    src_load.start()
    front_load.wait()
    src_load.wait()

    def add_blocks(ch, first, last):
        rows = pl.ds(ch * RC, RC)

        @pl.loop(first, last, unroll=2)
        def _(p):
            at = pl.ds(pl.multiple_of(p * BS, BS), BS)
            one = recvs[ch][src_s[0, p, 0]].astype(F32)
            two = recvs[ch][src_s[1, p, 0]].astype(F32)
            total = front_v[rows, at].astype(F32) + one + two
            work[rows, at] = total
            fb[rows, at] = total.astype(BF16)

    def wait_blocks(ch):
        @pl.loop(1, NO)
        def _(k):
            q = lax.rem(o + k, NO)
            arrived(recvs[ch].at[pl.ds(1 + 4 * q, 4)], ra.at[ch, q])

    def send_rows(ch, w, cols):
        src = fb.at[pl.ds(ch * RC, RC), pl.ds(first_col(w), cols)]
        dst = u.at[pl.ds(pl.multiple_of(r * ROWS + ch * RC, RC), RC), pl.ds(0, cols)]
        return src, dst

    def scatter(ch):
        @pl.when(r < 8)
        def _():
            @pl.loop(0, NW)
            def _(t):
                w = lax.rem(r + t, NW)

                def act(cols):
                    src, dst = send_rows(ch, w, cols)

                    @pl.when(w == r)
                    def _():
                        pltpu.make_async_copy(src, dst, rs.at[ch, lax.rem(r, 8)]).start()

                    @pl.when(w != r)
                    def _():
                        remote(src, dst, ss.at[ch, w], rs.at[ch, lax.rem(r, 8)], at_row(w)).start()

                by_width(w, act)

    rank_row = lax.broadcasted_iota(jnp.int32, (RM, BS), 0)

    def basis(k):
        return jnp.where(rank_row < ranks[0:1, k : k + 1], bases[...].astype(F32), 0.0)

    def order(k):
        ordered = nt(coef[k], one_hot[k]).astype(BF16)
        at = pl.ds(pl.multiple_of(jnp.maximum(r - 4 * (k + 1), 0) * RM, RM), RM)
        if k == 0:
            gm0[:, 0:PW] = ordered
            gm0[:, PW : PW + BS] = basis(k).astype(BF16)
        else:
            gm1[...] = ordered

        @pl.when(r >= 4 * (k + 1))
        def _():
            (g0, g1)[k][at, :] = (gm0, gm1)[k][...]

    def send_coef(k, q):
        return remote(coef.at[k], coef.at[k], sc.at[k, q], rcv.at[k], {"col": q})

    def send_pair(k):
        return remote(coef.at[k], coef.at[k], sc.at[k, 0], rcv.at[k], {"sub": 1 - s})

    def pass_coef(k):
        @pl.when(o == 0)
        def _():
            @pl.loop(1, ZS)
            def _(t):
                step = jnp.where(lax.rem(t, 2) == 1, ZS // 2 - t // 2, ZS // 2 + t // 2)
                send_coef(k, step).start()

        @pl.when(s == 0)
        def _():
            send_pair(k).start()

    def send_panel(i):
        return remote(
            fb.at[:, pl.ds(PW, PW)], u0p.at[pl.ds(pl.multiple_of(lax.rem(r, 4) * ROWS, ROWS), ROWS), :],
            su.at[i], ru.at[lax.rem(r, 4)], at_row(i),
        )

    def slot(k, i):
        return (g0, g1)[k].at[pl.ds(pl.multiple_of((i - 4 * (k + 1)) * RM, RM), RM), :]

    def send_order(k, w):
        at = pl.ds(pl.multiple_of(jnp.maximum(r - 4 * (k + 1), 0) * RM, RM), RM)
        return remote((gm0, gm1)[k], (g0, g1)[k].at[at, :], sg.at[k, w], rg.at[k, r], at_row(w))

    def sends_order(k, w):
        return (r >= 4 * (k + 1)) & (lax.rem(r, 2) == s) & (r != w)

    def share(k):
        @pl.loop(1, NW)
        def _(t):
            w = lax.rem(r + t, NW)

            @pl.when(sends_order(k, w))
            def _():
                send_order(k, w).start()

    def send_sibling(k, i):
        return remote(slot(k, i), slot(k, i), sf.at[k, i], rg.at[k, i], {"sub": 1 - s})

    def exchange(k):
        @pl.loop(4 * (k + 1), 16)
        def _(i):
            @pl.when((r != i) & (s == lax.rem(i, 2)))
            def _():
                arrived(slot(k, i), rg.at[k, i])
                send_sibling(k, i).start()

    def exchanged(k):
        @pl.loop(4 * (k + 1), 16)
        def _(i):
            @pl.when((r != i) & (s != lax.rem(i, 2)))
            def _():
                arrived(slot(k, i), rg.at[k, i])

    @pl.when(o == 0)
    def _():
        for ch in range(NCH):
            wait_blocks(ch)
        for ch in range(NCH):
            add_blocks(ch, 0, 8)

        @pl.when(r < 4)
        def _():
            @pl.loop(4, 16)
            def _(i):
                send_panel(i).start()

        inv_load.wait()
        coef[0] = mm_high(mm_high(basis(0), work[:, 0:PW]), inv_v[0]).astype(BF16)
        pass_coef(0)
        order(0)
        share(0)
        for ch in range(NCH):
            add_blocks(ch, 8, PB)
        p1[...] = work[:, PW : 2 * PW]

        @pl.when(r >= 4)
        def _():
            for i in range(4):
                arrived(u0p.at[pl.ds(i * ROWS, ROWS), :], ru.at[i])
            reduced = mm(gm0[:, 0:PW], u0p[...]).astype(BF16)
            p1[...] = p1[...] - mm(transposed(basis(0)).astype(BF16), reduced)

        coef[1] = mm_high(mm_high(basis(1), p1[...]), inv_v[1]).astype(BF16)
        pass_coef(1)
        send_chunk(2)
        send_chunk(3)
        order(1)
        share(1)
        for ch in range(NCH):
            scatter(ch)
        exchange(0)

    @pl.when(o != 0)
    def _():
        inv_load.wait()
        arrived(coef.at[0], rcv.at[0])
        pass_coef(0)
        order(0)
        share(0)
        for ch in range(NCH - 1):
            wait_blocks(ch)
            add_blocks(ch, 0, PB)
            scatter(ch)
        exchange(0)
        wait_blocks(NCH - 1)
        add_blocks(NCH - 1, 0, PB)
        scatter(NCH - 1)
        arrived(coef.at[1], rcv.at[1])
        pass_coef(1)
        order(1)
        share(1)

    coef_copy = pltpu.make_async_copy(coef, coef_out.at[:, 0], s_coef)
    coef_copy.start()

    def got_rows(first, last):
        def act(cols):
            @pl.loop(first, last)
            def _(i):
                for ch in range(NCH):
                    rows = pl.ds(pl.multiple_of(i * ROWS + ch * RC, RC), RC)
                    arrived(u.at[rows, pl.ds(0, cols)], rs.at[ch, i])

        by_width(r, act)

    def send_reduced(k, i, cols):
        src = (r0, r1)[k].at[pl.ds(pl.multiple_of((i - 4 * (k + 1)) * RM, RM), RM), pl.ds(0, cols)]
        dst = rbuf.at[pl.ds(k * RM, RM), pl.ds(first_col(r), cols)]
        return src, dst

    def give(k, first):
        def act(cols):
            @pl.loop(0, 4)
            def _(t):
                i = first + lax.rem(r + t, 4)
                src, dst = send_reduced(k, i, cols)

                @pl.when(r == i)
                def _():
                    pltpu.make_async_copy(src, dst, rr.at[k, r]).start()

                @pl.when(r != i)
                def _():
                    remote(src, dst, sr.at[k, i], rr.at[k, r], at_row(i)).start()

        by_width(r, act)

    exchanged(0)
    got_rows(0, 4)

    @pl.loop(0, 3)
    def _(t):
        at = pl.ds(pl.multiple_of(t * 256, 256), 256)
        r0[at, :] = mm(g0[at, 0:PW], u[0:PW, :]).astype(BF16)
        give(0, 4 + 4 * t)

    exchange(1)
    got_rows(4, 8)

    @pl.loop(0, 4)
    def _(i):
        ranks_at = pl.ds(pl.multiple_of(i * RM, RM), RM)
        b_t = transposed(g0[ranks_at, PW : PW + BS]).astype(BF16)
        rows = pl.ds(pl.multiple_of(PW + i * ROWS, ROWS), ROWS)
        u[rows, :] = (u[rows, :].astype(F32) - mm(b_t, r0[ranks_at, :])).astype(BF16)

    exchanged(1)

    @pl.loop(0, 2)
    def _(t):
        at = pl.ds(pl.multiple_of(t * 256, 256), 256)
        r1[at, :] = mm(g1[at, :], u[PW : 2 * PW, :]).astype(BF16)
        give(1, 8 + 4 * t)

    def each_part(act):
        @pl.loop(0, NW)
        def _(w):
            by_width(w, lambda cols: act(w, cols))

    def write(w, cols, src):
        at = pl.ds(first_col(w), cols)
        return pltpu.make_async_copy(src.at[:, at], out.at[:, at], so.at[w])

    @pl.when(r < 4)
    def _():
        each_part(lambda w, cols: write(w, cols, fb).start())

    def apply(count):
        b_t = transposed(jnp.concatenate([basis(0), basis(1)][:count], axis=0)).astype(BF16)

        def act(w, cols):
            at = pl.ds(first_col(w), cols)
            for k in range(count):
                arrived(rbuf.at[pl.ds(k * RM, RM), at], rr.at[k, w])
            outv[:, at] = (work[:, at] - mm(b_t, rbuf[0 : count * RM, at])).astype(BF16)
            write(w, cols, outv).start()

        each_part(act)

    @pl.when((r >= 4) & (r < 8))
    def _():
        apply(1)

    @pl.when(r >= 8)
    def _():
        apply(2)

    each_part(lambda w, cols: write(w, cols, outv).wait())
    coef_copy.wait()

    @pl.loop(1, NO)
    def _(k):
        q = lax.rem(o + k, NO)
        send_places(q).wait_send()
        for ch in range(NCH):
            send_blocks(ch, q).wait_send()

    @pl.when((o == 0) & (r < 4))
    def _():
        @pl.loop(4, 16)
        def _(i):
            send_panel(i).wait_send()

    for k in range(2):

        @pl.when(o == 0)
        def _():
            @pl.loop(1, ZS)
            def _(q):
                send_coef(k, q).wait_send()

        @pl.when(s == 0)
        def _():
            send_pair(k).wait_send()

        @pl.loop(0, NW)
        def _(w):
            @pl.when(sends_order(k, w))
            def _():
                send_order(k, w).wait_send()

        @pl.loop(4 * (k + 1), 16)
        def _(i):
            @pl.when((r != i) & (s == lax.rem(i, 2)))
            def _():
                send_sibling(k, i).wait_send()

        def sent(cols, k=k):
            @pl.loop(4 * (k + 1), 16)
            def _(i):
                src, dst = send_reduced(k, i, cols)

                @pl.when(r != i)
                def _():
                    remote(src, dst, sr.at[k, i], rr.at[k, r], at_row(i)).wait_send()

        by_width(r, sent)

    @pl.when(r < 8)
    def _():
        @pl.loop(1, NW)
        def _(t):
            w = lax.rem(r + t, NW)

            def act(cols):
                for ch in range(NCH):
                    src, dst = send_rows(ch, w, cols)
                    remote(src, dst, ss.at[ch, w], rs.at[ch, lax.rem(r, 8)], at_row(w)).wait_send()

            by_width(w, act)


def local(front, child_update, col_map, pivots, diag_inverse, ranks, bases):
    anywhere = pl.BlockSpec(memory_space=pl.ANY)
    dma = pltpu.SemaphoreType.DMA
    scratch = [
        pltpu.VMEM((1, KB), jnp.int32),
        pltpu.VMEM((2, PW), jnp.int32),
        pltpu.VMEM((1, 2), jnp.int32),
        pltpu.VMEM((RM, BS), BF16),
        pltpu.VMEM((2, PW, PW), BF16),
        pltpu.VMEM((NCH, RC, KB * BS), BF16),
        [pltpu.VMEM((KB, RC, BS), BF16) for _ in range(NCH)],
        pltpu.VMEM((ROWS, COLS), BF16),
        pltpu.VMEM((2, PW, PW), F32),
        pltpu.VMEM((NCH, KB, RC, BS), BF16),
        [pltpu.VMEM((KB + 1, RC, BS), BF16) for _ in range(NCH)],
        pltpu.VMEM((8, BS), jnp.int32),
        pltpu.VMEM((NO, 8, BS), jnp.int32),
        pltpu.VMEM((8, BS), jnp.int32),
        pltpu.SMEM((8, BS), jnp.int32),
        pltpu.VMEM((2, 56, BS), jnp.int32),
        pltpu.SMEM((2, 56, BS), jnp.int32),
        pltpu.VMEM((ROWS, COLS), F32),
        pltpu.VMEM((ROWS, COLS), BF16),
        pltpu.VMEM((ROWS, PW), F32),
        pltpu.VMEM((PW, PW), BF16),
        pltpu.VMEM((2, RM, PW), BF16),
        pltpu.VMEM((RM, PW + BS), BF16),
        pltpu.VMEM((RM, PW), BF16),
        pltpu.VMEM((12 * RM, PW + BS), BF16),
        pltpu.VMEM((8 * RM, PW), BF16),
        pltpu.VMEM((2 * PW, WC), BF16),
        pltpu.VMEM((12 * RM, WC), BF16),
        pltpu.VMEM((8 * RM, WC), BF16),
        pltpu.VMEM((2 * RM, COLS), BF16),
        pltpu.VMEM((ROWS, COLS), BF16),
        dma((NCH,)), dma((6,)), dma((2,)),
        dma((NCH, NO)), dma((NCH, NO)), dma((NO,)), dma((NO,)),
        dma((16,)), dma((4,)),
        dma((2, 8)), dma((2,)),
        dma((2, NW)), dma((2, 16)), dma((2, 16)),
        dma((NCH, NW)), dma((NCH, 8)),
        dma((2, 16)), dma((2, NW)),
        dma((NW,)), dma(()),
    ]
    return pl.pallas_call(
        kernel,
        out_shape=(
            jax.ShapeDtypeStruct((ROWS, COLS), BF16),
            jax.ShapeDtypeStruct((2, 1, RM, PW), BF16),
        ),
        in_specs=[anywhere] * 7,
        out_specs=(anywhere, anywhere),
        scratch_shapes=scratch,
        compiler_params=pltpu.CompilerParams(
            collective_id=0, has_side_effects=True, vmem_limit_bytes=60 * 1024 * 1024
        ),
        cost_estimate=pl.CostEstimate(flops=1_200_000_000, bytes_accessed=8_000_000, transcendentals=0),
    )(col_map.reshape(1, KB), pivots, ranks.reshape(1, 2), bases, child_update, front, diag_inverse)


def solution(mesh):
    return jax.shard_map(
        local,
        mesh=mesh,
        in_specs=(
            P("row", ("sub", "col")),
            P("row", ("sub", "col")),
            P(("sub", "col")),
            P(),
            P(),
            P(None, "row"),
            P(None, "row"),
        ),
        out_specs=(P("row", ("sub", "col")), P(None, "row", None, None)),
        check_vma=False,
    )
```

time: 139 us -> 111 us (0.80)
  the two profiles are of different devices: /device:TPU:159 before, /device:TPU:56 now
where the time goes in v2:
time: 111 us
  Pallas kernels  107 us (96%)
  local copies, waits for them, and re-layouts  3.39 us (3%)
    pallas_call x1, Pallas kernels, local(): pl.pallas_call(kernel, out_shape=(jax.ShapeDtypeStruct((ROWS, COLS), BF16...  107 us
    unnamed x4, local copies, waits for them, and re-layouts  3.39 us

profile of v2, /device:TPU:56, one launch (start us, length us, event | category | flops | bytes accessed | tf_op | source)
XLA Modules:
  0.0 110.8 jit_solution(2337820693059643094)
XLA Ops:
  0.6 106.8 %shard_map.86 = (bf16[128,6400]{1,0:T(8,128)(2,1)}, bf16[2,1,64,512]{3,2,1,0:T(8,128)(2,1)}) custom-call(s32[1,64]{1,0:T(1,128)} %bitcast.2, s32[2,512]{1,0:T(2,128)} %piv_h.1, s32[1,2]{1,0:T(1,128)} %bitcast.3, bf16[64,128]{1,0:T(8,128)(2,1)} %bases_h.1, bf16[128,8192]{1,0:T(8,128)(2,1)} %child.1, bf16[128,6400]{1,0:T(8,128)(2,1)} %front.1, f32[2,512,512]{2,1,0:T(8,128)} %inv.1), custom_call_target="tpu_custom_call" | custom-call | flops 1200000000 | bytes 8000000 | tf_op jit(solution)/shard_map/pallas_call | solution.py:610
  107.4 0.0 copy-start
  107.4 2.7 %copy.11 = bf16[128,6400]{1,0:T(8,128)(2,1)} copy(bf16[128,6400]{1,0:T(8,128)(2,1)} %get-tuple-element.4) | data formatting | bytes 3276800
  110.2 0.0 copy-done
  110.2 0.7 copy.12
Async XLA Ops:
  107.4 2.7 %copy-start = (bf16[2,1,64,512]{3,2,1,0:T(8,128)(2,1)S(1)}, bf16[2,1,64,512]{3,2,1,0:T(8,128)(2,1)}, u32[]{:S(2)}) copy-start(bf16[2,1,64,512]{3,2,1,0:T(8,128)(2,1)} %get-tuple-element.5) | copy-start | bytes 393220

commit v3 on v2

--- a/solution.py
+++ b/solution.py
@@ -153,22 +153,9 @@
     def send_chunk(ch):
         @pl.loop(0, NO)
         def _(t):
-            if ch == 0:
-
-                @pl.when(lax.rem(t, 4) == 0)
-                def _():
-                    for early in range(NCH):
-
-                        @pl.when(t == 4 * early)
-                        def _():
-                            pack(early, 0)
-
-                            @pl.when(o != 0)
-                            def _():
-                                send_blocks(early, 0).start()
-
             step = t // 2
-            shift = jnp.where(lax.rem(step, 2) == 1, (step + 1) // 2, ZS - step // 2)
+            base = 0 if ch == NCH - 1 else ZS // 2
+            shift = jnp.where(lax.rem(step, 2) == 1, base + (step + 1) // 2, base + ZS - step // 2)
             q = lax.rem(s + lax.rem(t, 2), 2) * ZS + lax.rem(c + shift, ZS)
 
             @pl.when(q != 0)
@@ -182,20 +169,24 @@
         for j in range(4):
             recvs[ch][1 + 4 * o + j] = outbuf[ch, 4 * o + j]
 
-    send_chunk(0)
-
-    @pl.when(o == 0)
-    def _():
-        for ch in range(1, NCH):
+    for ch in range(NCH):
+        pack(ch, 0)
+
+        @pl.when(o != 0)
+        def _(ch=ch):
+            send_blocks(ch, 0).start()
+
+        @pl.when(o == 0)
+        def _(ch=ch):
             for j in range(4):
                 recvs[ch][1 + j] = outbuf[ch, j]
 
-    send_chunk(1)
+    send_chunk(0)
 
     @pl.when(o != 0)
     def _():
-        send_chunk(2)
-        send_chunk(3)
+        for ch in range(1, NCH):
+            send_chunk(ch)
 
     for load in small[1:]:
         load.wait()
@@ -292,10 +283,8 @@
     def pass_coef(k):
         @pl.when(o == 0)
         def _():
-            @pl.loop(1, ZS)
-            def _(t):
-                step = jnp.where(lax.rem(t, 2) == 1, ZS // 2 - t // 2, ZS // 2 + t // 2)
-                send_coef(k, step).start()
+            for q in (4, 5, 3, 6, 1, 7, 2):
+                send_coef(k, jnp.int32(q)).start()
 
         @pl.when(s == 0)
         def _():
@@ -362,8 +351,11 @@
         pass_coef(0)
         order(0)
         share(0)
+        send_chunk(1)
+        send_chunk(2)
         for ch in range(NCH):
             add_blocks(ch, 8, PB)
+            scatter(ch)
         p1[...] = work[:, PW : 2 * PW]
 
         @pl.when(r >= 4)
@@ -375,12 +367,9 @@
 
         coef[1] = mm_high(mm_high(basis(1), p1[...]), inv_v[1]).astype(BF16)
         pass_coef(1)
-        send_chunk(2)
         send_chunk(3)
         order(1)
         share(1)
-        for ch in range(NCH):
-            scatter(ch)
         exchange(0)
 
     @pl.when(o != 0)
@@ -390,14 +379,22 @@
         pass_coef(0)
         order(0)
         share(0)
-        for ch in range(NCH - 1):
-            wait_blocks(ch)
-            add_blocks(ch, 0, PB)
-            scatter(ch)
+
+        @pl.when(r < 8)
+        def _():
+            for ch in range(NCH - 1):
+                wait_blocks(ch)
+                add_blocks(ch, 0, PB)
+                scatter(ch)
+
         exchange(0)
-        wait_blocks(NCH - 1)
-        add_blocks(NCH - 1, 0, PB)
-        scatter(NCH - 1)
+
+        @pl.when(r < 8)
+        def _():
+            wait_blocks(NCH - 1)
+            add_blocks(NCH - 1, 0, PB)
+            scatter(NCH - 1)
+
         arrived(coef.at[1], rcv.at[1])
         pass_coef(1)
         order(1)
@@ -465,6 +462,62 @@
         r1[at, :] = mm(g1[at, :], u[PW : 2 * PW, :]).astype(BF16)
         give(1, 8 + 4 * t)
 
+    @pl.when((o != 0) & (r >= 8))
+    def _():
+        for ch in range(NCH):
+            wait_blocks(ch)
+            add_blocks(ch, 0, PB)
+
+    @pl.loop(1, NO)
+    def _(k):
+        q = lax.rem(o + k, NO)
+        send_places(q).wait_send()
+        for ch in range(NCH):
+            send_blocks(ch, q).wait_send()
+
+    @pl.when((o == 0) & (r < 4))
+    def _():
+        @pl.loop(4, 16)
+        def _(i):
+            send_panel(i).wait_send()
+
+    for k in range(2):
+
+        @pl.when(o == 0)
+        def _():
+            @pl.loop(1, ZS)
+            def _(q):
+                send_coef(k, q).wait_send()
+
+        @pl.when(s == 0)
+        def _():
+            send_pair(k).wait_send()
+
+        @pl.loop(0, NW)
+        def _(w):
+            @pl.when(sends_order(k, w))
+            def _():
+                send_order(k, w).wait_send()
+
+        @pl.loop(4 * (k + 1), 16)
+        def _(i):
+            @pl.when((r != i) & (s == lax.rem(i, 2)))
+            def _():
+                send_sibling(k, i).wait_send()
+
+    @pl.when(r < 8)
+    def _():
+        @pl.loop(1, NW)
+        def _(t):
+            w = lax.rem(r + t, NW)
+
+            def act(cols):
+                for ch in range(NCH):
+                    src, dst = send_rows(ch, w, cols)
+                    remote(src, dst, ss.at[ch, w], rs.at[ch, lax.rem(r, 8)], at_row(w)).wait_send()
+
+            by_width(w, act)
+
     def each_part(act):
         @pl.loop(0, NW)
         def _(w):
@@ -501,42 +554,7 @@
     each_part(lambda w, cols: write(w, cols, outv).wait())
     coef_copy.wait()
 
-    @pl.loop(1, NO)
-    def _(k):
-        q = lax.rem(o + k, NO)
-        send_places(q).wait_send()
-        for ch in range(NCH):
-            send_blocks(ch, q).wait_send()
-
-    @pl.when((o == 0) & (r < 4))
-    def _():
-        @pl.loop(4, 16)
-        def _(i):
-            send_panel(i).wait_send()
-
     for k in range(2):
-
-        @pl.when(o == 0)
-        def _():
-            @pl.loop(1, ZS)
-            def _(q):
-                send_coef(k, q).wait_send()
-
-        @pl.when(s == 0)
-        def _():
-            send_pair(k).wait_send()
-
-        @pl.loop(0, NW)
-        def _(w):
-            @pl.when(sends_order(k, w))
-            def _():
-                send_order(k, w).wait_send()
-
-        @pl.loop(4 * (k + 1), 16)
-        def _(i):
-            @pl.when((r != i) & (s == lax.rem(i, 2)))
-            def _():
-                send_sibling(k, i).wait_send()
 
         def sent(cols, k=k):
             @pl.loop(4 * (k + 1), 16)
@@ -548,19 +566,6 @@
                     remote(src, dst, sr.at[k, i], rr.at[k, r], at_row(i)).wait_send()
 
         by_width(r, sent)
-
-    @pl.when(r < 8)
-    def _():
-        @pl.loop(1, NW)
-        def _(t):
-            w = lax.rem(r + t, NW)
-
-            def act(cols):
-                for ch in range(NCH):
-                    src, dst = send_rows(ch, w, cols)
-                    remote(src, dst, ss.at[ch, w], rs.at[ch, lax.rem(r, 8)], at_row(w)).wait_send()
-
-            by_width(w, act)
 
 
 def local(front, child_update, col_map, pivots, diag_inverse, ranks, bases):

time: 111 us -> 106 us (0.955)
  the two profiles are of different devices: /device:TPU:56 before, /device:TPU:250 now
where the time goes in v3:
time: 106 us
  Pallas kernels  102 us (96%)
  local copies, waits for them, and re-layouts  3.39 us (3%)
    pallas_call x1, Pallas kernels, local(): pl.pallas_call(kernel, out_shape=(jax.ShapeDtypeStruct((ROWS, COLS), BF16...  102 us
    unnamed x4, local copies, waits for them, and re-layouts  3.39 us

profile of v3, /device:TPU:250, one launch (start us, length us, event | category | flops | bytes accessed | tf_op | source)
XLA Modules:
  0.0 105.6 jit_solution(14157872094723390254)
XLA Ops:
  0.6 101.6 %shard_map.86 = (bf16[128,6400]{1,0:T(8,128)(2,1)}, bf16[2,1,64,512]{3,2,1,0:T(8,128)(2,1)}) custom-call(s32[1,64]{1,0:T(1,128)} %bitcast.2, s32[2,512]{1,0:T(2,128)} %piv_h.1, s32[1,2]{1,0:T(1,128)} %bitcast.3, bf16[64,128]{1,0:T(8,128)(2,1)} %bases_h.1, bf16[128,8192]{1,0:T(8,128)(2,1)} %child.1, bf16[128,6400]{1,0:T(8,128)(2,1)} %front.1, f32[2,512,512]{2,1,0:T(8,128)} %inv.1), custom_call_target="tpu_custom_call" | custom-call | flops 1200000000 | bytes 8000000 | tf_op jit(solution)/shard_map/pallas_call | solution.py:615
  102.2 0.0 copy-start
  102.2 2.7 %copy.11 = bf16[128,6400]{1,0:T(8,128)(2,1)} copy(bf16[128,6400]{1,0:T(8,128)(2,1)} %get-tuple-element.4) | data formatting | bytes 3276800
  105.0 0.0 copy-done
  105.0 0.7 copy.12
Async XLA Ops:
  102.2 2.7 %copy-start = (bf16[2,1,64,512]{3,2,1,0:T(8,128)(2,1)S(1)}, bf16[2,1,64,512]{3,2,1,0:T(8,128)(2,1)}, u32[]{:S(2)}) copy-start(bf16[2,1,64,512]{3,2,1,0:T(8,128)(2,1)} %get-tuple-element.5) | copy-start | bytes 393220

commit v4 on v3

--- a/solution.py
+++ b/solution.py
@@ -19,7 +19,7 @@
 NCH = 4
 RC = ROWS // NCH
 NW = 16
-SHARES = ((0, 2, 3), (2, 8, 2), (8, 16, 4))
+SHARES = ((0, 4, 2), (4, 8, 3), (8, 14, 4), (14, 16, 3))
 WC = 4 * BS
 F32 = jnp.float32
 BF16 = jnp.bfloat16
@@ -27,13 +27,21 @@
 
 
 def first_col(w):
-    return pl.multiple_of(jnp.where(w < 8, 2 * w + jnp.minimum(w, 2), 4 * w - 14) * BS, BS)
+    first, before = 0, 0
+    for start, end, blocks in SHARES:
+        first = jnp.where(w >= start, before + (w - start) * blocks, first)
+        before += (end - start) * blocks
+    return pl.multiple_of(first * BS, BS)
 
 
 def by_width(w, act):
-    for start, end, blocks in SHARES:
-
-        @pl.when((w >= start) & (w < end))
+    for blocks in sorted({share[2] for share in SHARES}):
+        mine = w < 0
+        for start, end, count in SHARES:
+            if count == blocks:
+                mine = mine | ((w >= start) & (w < end))
+
+        @pl.when(mine)
         def _():
             act(blocks * BS)
 

time: 106 us -> 101 us (0.953)
  the two profiles are of different devices: /device:TPU:250 before, /device:TPU:56 now
where the time goes in v4:
time: 101 us; the launch traced here: 100 us
  Pallas kernels  96.4 us (95%)
  local copies, waits for them, and re-layouts  3.39 us (3%)
    pallas_call x1, Pallas kernels, local(): pl.pallas_call(kernel, out_shape=(jax.ShapeDtypeStruct((ROWS, COLS), BF16...  96.4 us
    unnamed x4, local copies, waits for them, and re-layouts  3.39 us

profile of v4, /device:TPU:56, one launch (start us, length us, event | category | flops | bytes accessed | tf_op | source)
XLA Modules:
  0.0 100.5 jit_solution(10364398481130235672)
XLA Ops:
  0.6 96.4 %shard_map.86 = (bf16[128,6400]{1,0:T(8,128)(2,1)}, bf16[2,1,64,512]{3,2,1,0:T(8,128)(2,1)}) custom-call(s32[1,64]{1,0:T(1,128)} %bitcast.2, s32[2,512]{1,0:T(2,128)} %piv_h.1, s32[1,2]{1,0:T(1,128)} %bitcast.3, bf16[64,128]{1,0:T(8,128)(2,1)} %bases_h.1, bf16[128,8192]{1,0:T(8,128)(2,1)} %child.1, bf16[128,6400]{1,0:T(8,128)(2,1)} %front.1, f32[2,512,512]{2,1,0:T(8,128)} %inv.1), custom_call_target="tpu_custom_call" | custom-call | flops 1200000000 | bytes 8000000 | tf_op jit(solution)/shard_map/pallas_call | solution.py:623
  97.1 0.0 copy-start
  97.1 2.7 %copy.11 = bf16[128,6400]{1,0:T(8,128)(2,1)} copy(bf16[128,6400]{1,0:T(8,128)(2,1)} %get-tuple-element.4) | data formatting | bytes 3276800
  99.8 0.0 copy-done
  99.8 0.7 copy.12
Async XLA Ops:
  97.1 2.7 %copy-start = (bf16[2,1,64,512]{3,2,1,0:T(8,128)(2,1)S(1)}, bf16[2,1,64,512]{3,2,1,0:T(8,128)(2,1)}, u32[]{:S(2)}) copy-start(bf16[2,1,64,512]{3,2,1,0:T(8,128)(2,1)} %get-tuple-element.5) | copy-start | bytes 393220
